TPU v7x, 128 devices: a whole 4x4x4 slice. The times are simulated.
128 devices in a mesh: dom: 32 (over y, x, core), grp: 4 (over z).
Axes of the slice: x: 4, y: 4, z: 4, core: 2. Of those that a mesh axis runs over, the one named last changes fastest.
Arguments:
- encoded: float32 [65536, 1024], P(('dom', 'grp')), may hold values from -6 to 6
- owner_of: int32 [65536], P(('dom', 'grp')), may hold values from 0 to 65535, as said below
- nbr_blocks: int32 [512, 16], P(('dom', 'grp')), may hold values from 0 to 15, as said below
- nbr_count: int32 [512], P(('dom', 'grp')), may hold values from 1 to 16, as said below
- edge_weights: bfloat16 [512, 16, 128, 128], P(('dom', 'grp')), may hold values from 0.01 to 16
Outputs:
- propagated: bfloat16 [65536, 1024], P(('dom', 'grp'))
Inputs may be any that keep to these rules, and one draw needn't show every extreme that they name: owner_of is a permutation; the batch rows of each device go to the nodes of every device in equal numbers (512 / the device count to each), where device d owns nodes d * 512 to (d + 1) * 512 - 1. `nbr_blocks`: A partition group is the 2048 nodes of the devices that share a dom index; block g of a group is its nodes g * 128 to (g + 1) * 128 - 1. The first nbr_count[b] entries of row block b are distinct; later entries are padding and are ignored. `nbr_count`: some row block has exactly 16 live blocks.
All inputs are finite; a program needn't handle non-finite values.
Results may differ from a plain program's by a relative error of at most 0.005.
Values may be sent and summed in bfloat16 or wider, within the bound.
No kernel may reach another device: no remote copies, remote signals or barrier semaphores. Data moves between devices by JAX's collectives and lax.ppermute only.
A program may use at most 64 MiB of HBM per device.

v0:
```python
import jax
import jax.numpy as jnp
from jax import lax
from jax.sharding import PartitionSpec as P

STEPS = 2
mix_weight = 0.3


def propagate(base_rows, weight_table, list_table, count_table, panel_blocks, gather_panel):
    block_count, slot_count, block_size, _ = weight_table.shape
    live_table = jnp.arange(slot_count, dtype=jnp.int32)[None, :] < count_table[:, None]
    picks = (
        list_table[:, :, None] == jnp.arange(panel_blocks, dtype=jnp.int32)[None, None, :]
    ) & live_table[:, :, None]
    select = picks.astype(jnp.bfloat16)
    dense = jnp.einsum(
        "bkg,bkpq->bpgq", select, weight_table, preferred_element_type=jnp.float32
    ).astype(jnp.bfloat16)
    dense = dense.reshape(block_count * block_size, panel_blocks * block_size)
    degree = jnp.sum(dense, axis=1, dtype=jnp.float32)
    row_scale = lax.rsqrt(degree)[:, None]
    hidden = base_rows.astype(jnp.bfloat16)
    for step_index in range(STEPS):
        panel_rows = gather_panel(hidden)
        running = jnp.dot(dense, panel_rows, preferred_element_type=jnp.float32)
        hidden = (mix_weight * base_rows + (1.0 - mix_weight) * running * row_scale).astype(
            jnp.bfloat16
        )
    return hidden


def shards(encoded, owner_of, nbr_blocks, nbr_count, edge_weights):
    row_count, feat_width = encoded.shape
    block_count, slot_count, block_size, _ = edge_weights.shape
    target_dev = owner_of // row_count
    send_order = jnp.argsort(target_dev, stable=True)
    row_ids = jnp.arange(row_count, dtype=jnp.int32)
    send_pick = (send_order[:, None] == row_ids[None, :]).astype(jnp.float32)
    outgoing = jnp.dot(
        send_pick, encoded, precision=lax.Precision.HIGHEST, preferred_element_type=jnp.float32
    )
    places = jnp.take(owner_of, send_order, axis=0)
    arrived, where_to = (
        lax.all_to_all(
            outgoing.astype(jnp.bfloat16), ("dom", "grp"), split_axis=0, concat_axis=0, tiled=True
        ).astype(outgoing.dtype),
        lax.all_to_all(places, ("dom", "grp"), split_axis=0, concat_axis=0, tiled=True),
    )
    place_pick = (row_ids[:, None] == (where_to % row_count)[None, :]).astype(jnp.float32)
    base_rows = jnp.dot(
        place_pick, arrived, precision=lax.Precision.HIGHEST, preferred_element_type=jnp.float32
    )

    def group_panel(hidden):
        return lax.all_gather(hidden, "grp", axis=0, tiled=True)

    panel_blocks = block_count * lax.axis_size("grp")
    return propagate(base_rows, edge_weights, nbr_blocks, nbr_count, panel_blocks, group_panel)


def solution(mesh):
    return jax.shard_map(
        shards,
        mesh=mesh,
        in_specs=(
            P(("dom", "grp"), None),
            P(("dom", "grp")),
            P(("dom", "grp"), None),
            P(("dom", "grp")),
            P(("dom", "grp"), None, None, None),
        ),
        out_specs=P(("dom", "grp"), None),
        check_vma=False,
    )
```

profile of v0, /device:TPU:1, one launch (start us, length us, event | category | flops | bytes accessed | tf_op | source)
XLA Modules:
  0.0 179.5 jit_solution(9671089370718514029)
XLA Ops:
  6.5 0.8 add_select_fusion.1
  7.4 3.8 %sort.17 = (s32[512]{0:T(512)}, s32[512]{0:T(512)S(1)}) sort(s32[512]{0:T(512)S(1)} %add_select_fusion.1, s32[512]{0:T(512)S(1)} %iota.22), dimensions={0}, to_apply=%region_0.1 | sort | flops 4608 | bytes 8192 | tf_op jit(solution)/shard_map/jit(argsort)/sort | solution.py:37
  11.2 3.6 %gather_fusion = s32[512]{0:T(512)S(1)} fusion(s32[512]{0:T(512)} %param.6, s32[1024]{0:T(1024)S(1)} %pad_clamp_fusion), kind=kCustom, calls=%fused_computation | custom fusion | bytes 6144 | tf_op jit(solution)/shard_map/jit(_take)/gather | solution.py:43
  14.8 0.7 select_n.37
  15.5 11.5 %all-to-all-start = ((s32[128,4,1]{1,2,0:T(1,128)}), s32[128,4,1]{1,2,0:T(1,128)S(1)}, u32[]{:S(2)}, u32[]{:S(2)}) async-start(s32[128,4,1]{1,2,0:T(1,128)} %bitcast), calls=%async_computation | async-start | bytes 131072 | tf_op jit(solution)/shard_map/all_to_all | solution.py:48
  27.0 3.6 %convolution_convert_fusion = bf16[512,1024]{1,0:T(8,128)(2,1)S(1)} fusion(f32[512,1024]{1,0:T(8,128)} %param.5, s32[512]{0:T(512)S(1)} %get-tuple-element.6), kind=kOutput, calls=%fused_computation.13 | convolution fusion | flops 3222011904 | bytes 3147776 | tf_op jit(solution)/shard_map/dot_general | solution.py:40
  30.6 1.2 all_to_all.16
  31.8 4.8 %all-to-all-done = s32[128,4,1]{1,2,0:T(1,128)S(1)} async-done(((s32[128,4,1]{1,2,0:T(1,128)}), s32[128,4,1]{1,2,0:T(1,128)S(1)}, u32[]{:S(2)}, u32[]{:S(2)}) %all-to-all-start) | async-done | bytes 2080 | tf_op jit(solution)/shard_map/all_to_all | solution.py:48
  36.6 5.0 %all-to-all-start.1 = ((bf16[128,4,1024]{2,1,0:T(4,128)(2,1)}), bf16[128,4,1024]{2,1,0:T(4,128)(2,1)S(1)}, u32[]{:S(2)}, u32[]{:S(2)}) async-start(bf16[128,4,1024]{2,1,0:T(4,128)(2,1)} %all_to_all.16), calls=%async_computation.1 | async-start | bytes 2097152 | tf_op jit(solution)/shard_map/all_to_all | solution.py:45
  41.6 0.0 all-gather.3.cloned.1.call-start
  41.6 0.5 broadcast.84
  42.2 0.8 reduce.4
  43.0 0.1 all_to_all.15
  43.1 17.9 %all-to-all-done.1 = bf16[128,4,1024]{2,1,0:T(4,128)(2,1)S(1)} async-done(((bf16[128,4,1024]{2,1,0:T(4,128)(2,1)}), bf16[128,4,1024]{2,1,0:T(4,128)(2,1)S(1)}, u32[]{:S(2)}, u32[]{:S(2)}) %all-to-all-start.1) | async-done | bytes 1048608 | tf_op jit(solution)/shard_map/all_to_all | solution.py:45
  61.0 1.1 all_to_all.18
  62.1 3.7 %fusion.26 = (bf16[512,1024]{1,0:T(8,128)(2,1)}, f32[512,1024]{1,0:T(8,128)}) fusion(bf16[512,1024]{1,0:T(8,128)(2,1)} %all_to_all.18, s32[512]{0:T(512)S(1)} %add_select_fusion), kind=kOutput, calls=%fused_computation.40 | convolution fusion | flops 537657344 | bytes 4196352 | tf_op jit(solution)/shard_map/dot_general | solution.py:51
  65.8 0.0 all-gather.3.cloned.1.call-update
  65.8 0.2 all-gather.5.cloned.1.call-start
  66.1 0.1 iota_compare_fusion.5
  66.1 3.6 %convert_reduce_fusion = (f32[4,128]{1,0:T(4,128)S(1)}, bf16[4,16,128,128]{3,1,2,0:T(8,128)(2,1)}) fusion(bf16[4,16,128,128]{3,2,1,0:T(8,128)(2,1)S(1)} %copy-done, s32[4,16]{1,0:T(4,128)S(1)} %copy-done.1, pred[4,16]{1,0:T(4,128)(4,1)S(1)} %iota_compare_fusion.5), kind=kOutput, calls=%fused_computation.1 | convolution fusion | flops 36701696 | bytes 4196672 | tf_op jit(solution)/shard_map/bkg,bkpq->bpgq/dot_general | solution.py:17
  69.8 40.5 %all-gather.3.cloned.1.call-done = bf16[2048,1024]{1,0:T(8,128)(2,1)} async-done(((bf16[512,1024]{1,0:T(8,128)(2,1)}), bf16[2048,1024]{1,0:T(8,128)(2,1)}) %all-gather.3.cloned.1.call-update) | async-done | bytes 4194320 | tf_op jit(solution)/shard_map/all_gather | solution.py:56
  110.2 6.8 %add_convert_fusion.1 = bf16[512,1024]{1,0:T(8,128)(2,1)} fusion(f32[512,1024]{1,0:T(8,128)} %get-tuple-element.8, bf16[2048,1024]{1,0:T(8,128)(2,1)} %all-gather.3.cloned.1.call-done, bf16[64,8,16,128]{3,2,1,0:T(8,128)(2,1)} %bitcast.28, f32[512]{0:T(512)S(1)} %multiply_bitcast_fusion), kind=kOutput, calls=%fused_computation.9 | convolution fusion | flops 2149580800 | bytes 9439232 | tf_op jit(solution)/shard_map/dot_general | solution.py:26
  117.0 48.8 %all-gather.5.cloned.1.call-done = bf16[2048,1024]{1,0:T(8,128)(2,1)} async-done(((bf16[512,1024]{1,0:T(8,128)(2,1)}), bf16[2048,1024]{1,0:T(8,128)(2,1)}) %all-gather.5.cloned.1.call-update) | async-done | bytes 4194320 | tf_op jit(solution)/shard_map/all_gather | solution.py:56
  165.9 6.8 %add_convert_fusion = bf16[512,1024]{1,0:T(8,128)(2,1)} fusion(f32[512,1024]{1,0:T(8,128)} %get-tuple-element.8, bf16[2048,1024]{1,0:T(8,128)(2,1)} %all-gather.5.cloned.1.call-done, bf16[64,8,16,128]{3,2,1,0:T(8,128)(2,1)} %bitcast.29, f32[512]{0:T(512)S(1)} %multiply_bitcast_fusion), kind=kOutput, calls=%fused_computation.8 | convolution fusion | flops 2149580800 | bytes 9439232 | tf_op jit(solution)/shard_map/dot_general | solution.py:26
  (13 shorter events, 0.1 us)
Async XLA Ops:
  6.5 59.6 %copy-start = (bf16[4,16,128,128]{3,2,1,0:T(8,128)(2,1)S(1)}, bf16[4,16,128,128]{3,2,1,0:T(8,128)(2,1)}, u32[]{:S(2)}) copy-start(bf16[4,16,128,128]{3,2,1,0:T(8,128)(2,1)} %param.9) | copy-start | bytes 6291460
  15.5 21.1 %all-to-all-start = ((s32[128,4,1]{1,2,0:T(1,128)}), s32[128,4,1]{1,2,0:T(1,128)S(1)}, u32[]{:S(2)}, u32[]{:S(2)}) async-start(s32[128,4,1]{1,2,0:T(1,128)} %bitcast), calls=%async_computation | async-start | bytes 131072 | tf_op jit(solution)/shard_map/all_to_all | solution.py:48
  36.6 24.4 %all-to-all-start.1 = ((bf16[128,4,1024]{2,1,0:T(4,128)(2,1)}), bf16[128,4,1024]{2,1,0:T(4,128)(2,1)S(1)}, u32[]{:S(2)}, u32[]{:S(2)}) async-start(bf16[128,4,1024]{2,1,0:T(4,128)(2,1)} %all_to_all.16), calls=%async_computation.1 | async-start | bytes 2097152 | tf_op jit(solution)/shard_map/all_to_all | solution.py:45
  41.6 68.6 %all-gather.3.cloned.1.call-start = ((), (), s32[]{:S(2)}) async-start(), calls=%async_computation.2 | async-start | bytes 5242880 | tf_op jit(solution)/shard_map/all_gather | solution.py:56
  62.1 4.0 %copy-start.2 = (s32[4]{0:T(128)S(1)}, s32[4]{0:T(128)}, u32[]{:S(2)}) copy-start(s32[4]{0:T(128)} %param.8) | copy-start | bytes 52
  62.1 4.0 %copy-start.1 = (s32[4,16]{1,0:T(4,128)S(1)}, s32[4,16]{1,0:T(4,128)}, u32[]{:S(2)}) copy-start(s32[4,16]{1,0:T(4,128)} %param.7) | copy-start | bytes 772
  65.8 100.0 %all-gather.5.cloned.1.call-start = ((), (), s32[]{:S(2)}) async-start(), calls=%async_computation.3 | async-start | bytes 5242880 | tf_op jit(solution)/shard_map/all_gather | solution.py:56
Sparse Core Ops, SparseCore 0:
  65.9 44.2 all-gather.2
  117.2 48.6 all-gather.4
where the time goes:
time: 180 us; the launch traced here: 179 us
  waiting for transfers between devices  112 us (62%)
  matrix products  24.5 us (14%)
  starting transfers between devices  16.8 us (9%)
  between operations  13.5 us (8%)
  local copies, waits for them, and re-layouts  7.3 us (4%)
  other arithmetic  5.51 us (3%)
    all_gather x2, waiting for transfers between devices, group_panel(): return lax.all_gather(hidden, 'grp', axis=0, tiled=True)  89.3 us
    all_to_all x1, waiting for transfers between devices, shards(): lax.all_to_all(outgoing.astype(jnp.bfloat16), ('dom', 'grp'), split_axis=...  17.9 us
    dot_general x2, matrix products, propagate(): running = jnp.dot(dense, panel_rows, preferred_element_type=jnp.float32)  13.6 us
    all_to_all x1, starting transfers between devices, shards(): lax.all_to_all(places, ('dom', 'grp'), split_axis=0, concat_axis=0, tiled...  11.5 us
    all_to_all x1, starting transfers between devices, shards(): lax.all_to_all(outgoing.astype(jnp.bfloat16), ('dom', 'grp'), split_axis=...  4.99 us
    all_to_all x1, waiting for transfers between devices, shards(): lax.all_to_all(places, ('dom', 'grp'), split_axis=0, concat_axis=0, tiled...  4.77 us
    sort x1, other arithmetic, shards(): send_order = jnp.argsort(target_dev, stable=True)  3.77 us
    dot_general x1, matrix products, shards(): jnp.dot(place_pick, arrived, precision=lax.Precision.HIGHEST, preferred_e...  3.69 us
  transfers between devices with their start and end apart: 4, of which 4 were waited for; matrix products, arithmetic and copies ran while one was open for 5% of the time, Pallas kernels for 0%

commit v1 on v0

--- a/solution.py
+++ b/solution.py
@@ -53,7 +53,9 @@
     )
 
     def group_panel(hidden):
-        return lax.all_gather(hidden, "grp", axis=0, tiled=True)
+        return jnp.concatenate(
+            lax.all_to_all(jnp.stack([hidden] * lax.axis_size("grp")), "grp", 0, 0), axis=0
+        )
 
     panel_blocks = block_count * lax.axis_size("grp")
     return propagate(base_rows, edge_weights, nbr_blocks, nbr_count, panel_blocks, group_panel)

time: 180 us -> 176 us (0.978)
  blocking collectives: 0 us -> 50.1 us
  waiting for transfers between devices: 112 us -> 67.6 us
  between operations: 13.5 us -> 0.1 us
  matrix products: 24.5 us -> 19.7 us
  starting transfers between devices: 16.8 us -> 21.4 us
  local copies, waits for them, and re-layouts: 7.3 us -> 10.5 us
    all_gather x2 -> x0, waiting for transfers between devices: 89.3 us -> none  [group_panel(): return lax.all_gather(hidden, 'grp', axis=0, tiled=True)]
    all_to_all x0 -> x1, blocking collectives: none -> 50.1 us  [group_panel(): lax.all_to_all(jnp.stack([hidden] * lax.axis_size('grp')), 'grp', 0, 0)]
    all_to_all x0 -> x1, waiting for transfers between devices: none -> 44.9 us  [group_panel(): lax.all_to_all(jnp.stack([hidden] * lax.axis_size('grp')), 'grp', 0, 0)]
    all_to_all x0 -> x1, starting transfers between devices: none -> 4.99 us  [group_panel(): lax.all_to_all(jnp.stack([hidden] * lax.axis_size('grp')), 'grp', 0, 0)]
    dot_general x2, matrix products: 13.6 us -> 9.19 us  [propagate(): running = jnp.dot(dense, panel_rows, preferred_element_type=jnp.float32)]
    another operation x0 -> x2, local copies, waits for them, and re-layouts: none -> 3.13 us  [group_panel(): jnp.stack([hidden] * lax.axis_size('grp'))]
  transfers between devices with their start and end apart: 4 -> 3, of which waited for: 4 -> 3; matrix products, arithmetic and copies ran while one was open for 5% -> 5% of each run, Pallas kernels for 0% -> 0%
where the time goes in v1:
time: 176 us; the launch traced here: 175 us
  waiting for transfers between devices  67.6 us (38%)
  blocking collectives  50.1 us (28%)
  starting transfers between devices  21.4 us (12%)
  matrix products  19.7 us (11%)
  local copies, waits for them, and re-layouts  10.5 us (6%)
  other arithmetic  5.57 us (3%)
    all_to_all x1, blocking collectives, group_panel(): lax.all_to_all(jnp.stack([hidden] * lax.axis_size('grp')), 'grp', 0, 0)  50.1 us
    all_to_all x1, waiting for transfers between devices, group_panel(): lax.all_to_all(jnp.stack([hidden] * lax.axis_size('grp')), 'grp', 0, 0)  44.9 us
    all_to_all x1, waiting for transfers between devices, shards(): lax.all_to_all(outgoing.astype(jnp.bfloat16), ('dom', 'grp'), split_axis=...  17.8 us
    all_to_all x1, starting transfers between devices, shards(): lax.all_to_all(places, ('dom', 'grp'), split_axis=0, concat_axis=0, tiled...  11.5 us
    dot_general x2, matrix products, propagate(): running = jnp.dot(dense, panel_rows, preferred_element_type=jnp.float32)  9.19 us
    all_to_all x1, starting transfers between devices, group_panel(): lax.all_to_all(jnp.stack([hidden] * lax.axis_size('grp')), 'grp', 0, 0)  4.99 us
    all_to_all x1, starting transfers between devices, shards(): lax.all_to_all(outgoing.astype(jnp.bfloat16), ('dom', 'grp'), split_axis=...  4.93 us
    all_to_all x1, waiting for transfers between devices, shards(): lax.all_to_all(places, ('dom', 'grp'), split_axis=0, concat_axis=0, tiled...  4.84 us
  transfers between devices with their start and end apart: 3, of which 3 were waited for; matrix products, arithmetic and copies ran while one was open for 5% of the time, Pallas kernels for 0%

profile of v1, /device:TPU:1, one launch (start us, length us, event | category | flops | bytes accessed | tf_op | source)
XLA Modules:
  0.0 175.0 jit_solution(3496477674563621151)
XLA Ops:
  0.0 0.8 add_select_fusion.1
  0.8 3.8 %sort.17 = (s32[512]{0:T(512)}, s32[512]{0:T(512)S(1)}) sort(s32[512]{0:T(512)S(1)} %add_select_fusion.1, s32[512]{0:T(512)S(1)} %iota.22), dimensions={0}, to_apply=%region_0.1 | sort | flops 4608 | bytes 8192 | tf_op jit(solution)/shard_map/jit(argsort)/sort | solution.py:37
  4.6 3.6 %gather_fusion = s32[512]{0:T(512)S(1)} fusion(s32[512]{0:T(512)} %param.6, s32[1024]{0:T(1024)S(1)} %pad_clamp_fusion), kind=kCustom, calls=%fused_computation | custom fusion | bytes 6144 | tf_op jit(solution)/shard_map/jit(_take)/gather | solution.py:43
  8.3 0.7 select_n.37
  9.0 11.5 %all-to-all-start = ((s32[128,4,1]{1,2,0:T(1,128)}), s32[128,4,1]{1,2,0:T(1,128)S(1)}, u32[]{:S(2)}, u32[]{:S(2)}) async-start(s32[128,4,1]{1,2,0:T(1,128)} %bitcast), calls=%async_computation | async-start | bytes 131072 | tf_op jit(solution)/shard_map/all_to_all | solution.py:48
  20.5 3.6 %convolution_convert_fusion = bf16[512,1024]{1,0:T(8,128)(2,1)S(1)} fusion(f32[512,1024]{1,0:T(8,128)} %param.5, s32[512]{0:T(512)S(1)} %get-tuple-element.6), kind=kOutput, calls=%fused_computation.13 | convolution fusion | flops 3222011904 | bytes 3147776 | tf_op jit(solution)/shard_map/dot_general | solution.py:40
  24.1 1.2 all_to_all.22
  25.3 4.8 %all-to-all-done = s32[128,4,1]{1,2,0:T(1,128)S(1)} async-done(((s32[128,4,1]{1,2,0:T(1,128)}), s32[128,4,1]{1,2,0:T(1,128)S(1)}, u32[]{:S(2)}, u32[]{:S(2)}) %all-to-all-start) | async-done | bytes 2080 | tf_op jit(solution)/shard_map/all_to_all | solution.py:48
  30.1 4.9 %all-to-all-start.1 = ((bf16[128,4,1024]{2,1,0:T(4,128)(2,1)}), bf16[128,4,1024]{2,1,0:T(4,128)(2,1)S(1)}, u32[]{:S(2)}, u32[]{:S(2)}) async-start(bf16[128,4,1024]{2,1,0:T(4,128)(2,1)} %all_to_all.22), calls=%async_computation.1 | async-start | bytes 2097152 | tf_op jit(solution)/shard_map/all_to_all | solution.py:45
  35.1 0.6 broadcast.88
  35.7 0.8 reduce.4
  36.5 0.1 all_to_all.21
  36.6 17.8 %all-to-all-done.1 = bf16[128,4,1024]{2,1,0:T(4,128)(2,1)S(1)} async-done(((bf16[128,4,1024]{2,1,0:T(4,128)(2,1)}), bf16[128,4,1024]{2,1,0:T(4,128)(2,1)S(1)}, u32[]{:S(2)}, u32[]{:S(2)}) %all-to-all-start.1) | async-done | bytes 1048608 | tf_op jit(solution)/shard_map/all_to_all | solution.py:45
  54.5 1.1 all_to_all.24
  55.6 3.3 %fusion.26 = (bf16[512,1024]{1,0:T(8,128)(2,1)S(1)}, f32[512,1024]{1,0:T(8,128)}) fusion(bf16[512,1024]{1,0:T(8,128)(2,1)} %all_to_all.24, s32[512]{0:T(512)S(1)} %add_select_fusion), kind=kOutput, calls=%fused_computation.40 | convolution fusion | flops 537657344 | bytes 4196352 | tf_op jit(solution)/shard_map/dot_general | solution.py:51
  58.9 2.6 %stack.4 = bf16[4,512,1024]{2,1,0:T(8,128)(2,1)} broadcast(bf16[512,1024]{1,0:T(8,128)(2,1)S(1)} %get-tuple-element.7), dimensions={1,2} | broadcast | bytes 5242880 | tf_op jit(solution)/shard_map/stack | solution.py:57
  61.5 5.0 %all-to-all-start.2 = ((bf16[4,512,1024]{2,1,0:T(8,128)(2,1)}), bf16[4,512,1024]{2,1,0:T(8,128)(2,1)}, u32[]{:S(2)}, u32[]{:S(2)}) async-start(bf16[4,512,1024]{2,1,0:T(8,128)(2,1)} %stack.4), calls=%async_computation.2 | async-start | bytes 8388608 | tf_op jit(solution)/shard_map/all_to_all | solution.py:57
  66.5 0.1 iota_compare_fusion.5
  66.6 3.6 %convert_reduce_fusion = (f32[4,128]{1,0:T(4,128)S(1)}, bf16[4,16,128,128]{3,1,2,0:T(8,128)(2,1)}) fusion(bf16[4,16,128,128]{3,2,1,0:T(8,128)(2,1)S(1)} %copy-done, s32[4,16]{1,0:T(4,128)S(1)} %copy-done.3, pred[4,16]{1,0:T(4,128)(4,1)S(1)} %iota_compare_fusion.5), kind=kOutput, calls=%fused_computation.1 | convolution fusion | flops 36701696 | bytes 4196672 | tf_op jit(solution)/shard_map/bkg,bkpq->bpgq/dot_general | solution.py:17
  70.2 44.9 %all-to-all-done.2 = bf16[4,512,1024]{2,1,0:T(8,128)(2,1)} async-done(((bf16[4,512,1024]{2,1,0:T(8,128)(2,1)}), bf16[4,512,1024]{2,1,0:T(8,128)(2,1)}, u32[]{:S(2)}, u32[]{:S(2)}) %all-to-all-start.2) | async-done | bytes 4194336 | tf_op jit(solution)/shard_map/all_to_all | solution.py:57
  115.1 5.8 %add_convert_fusion.1 = bf16[512,1024]{1,0:T(8,128)(2,1)S(1)} fusion(f32[512,1024]{1,0:T(8,128)} %get-tuple-element.8, bf16[2048,1024]{1,0:T(8,128)(2,1)} %bitcast.4, bf16[64,8,16,128]{3,2,1,0:T(8,128)(2,1)} %bitcast.31, f32[512]{0:T(512)S(1)} %multiply_bitcast_fusion), kind=kOutput, calls=%fused_computation.9 | convolution fusion | flops 2149580800 | bytes 9439232 | tf_op jit(solution)/shard_map/dot_general | solution.py:26
  120.9 0.5 stack.5
  121.5 50.1 %all_to_all.31 = bf16[4,512,1024]{2,1,0:T(8,128)(2,1)S(1)} all-to-all(bf16[4,512,1024]{2,1,0:T(8,128)(2,1)S(1)} %stack.5), channel_id=1, replica_groups=mesh['dom'=32,'grp'=4] {'grp'}, dimensions={0} | all-to-all | bytes 8388608 | tf_op jit(solution)/shard_map/all_to_all | solution.py:57
  171.6 3.4 %add_convert_fusion = bf16[512,1024]{1,0:T(8,128)(2,1)} fusion(f32[512,1024]{1,0:T(8,128)S(1)} %copy-done.2, bf16[2048,1024]{1,0:T(8,128)(2,1)S(1)} %bitcast.30, bf16[64,8,16,128]{3,2,1,0:T(8,128)(2,1)S(1)} %bitcast.32, f32[512]{0:T(512)S(1)} %multiply_bitcast_fusion), kind=kOutput, calls=%fused_computation.8 | convolution fusion | flops 2149580800 | bytes 9439232 | tf_op jit(solution)/shard_map/dot_general | solution.py:26
  (16 shorter events, 0.1 us)
Async XLA Ops:
  0.0 66.6 %copy-start = (bf16[4,16,128,128]{3,2,1,0:T(8,128)(2,1)S(1)}, bf16[4,16,128,128]{3,2,1,0:T(8,128)(2,1)}, u32[]{:S(2)}) copy-start(bf16[4,16,128,128]{3,2,1,0:T(8,128)(2,1)} %param.9) | copy-start | bytes 6291460
  9.0 21.1 %all-to-all-start = ((s32[128,4,1]{1,2,0:T(1,128)}), s32[128,4,1]{1,2,0:T(1,128)S(1)}, u32[]{:S(2)}, u32[]{:S(2)}) async-start(s32[128,4,1]{1,2,0:T(1,128)} %bitcast), calls=%async_computation | async-start | bytes 131072 | tf_op jit(solution)/shard_map/all_to_all | solution.py:48
  30.1 24.4 %all-to-all-start.1 = ((bf16[128,4,1024]{2,1,0:T(4,128)(2,1)}), bf16[128,4,1024]{2,1,0:T(4,128)(2,1)S(1)}, u32[]{:S(2)}, u32[]{:S(2)}) async-start(bf16[128,4,1024]{2,1,0:T(4,128)(2,1)} %all_to_all.22), calls=%async_computation.1 | async-start | bytes 2097152 | tf_op jit(solution)/shard_map/all_to_all | solution.py:45
  61.5 5.0 %copy-start.4 = (s32[4]{0:T(128)S(1)}, s32[4]{0:T(128)}, u32[]{:S(2)}) copy-start(s32[4]{0:T(128)} %param.8) | copy-start | bytes 52
  61.5 5.1 %copy-start.3 = (s32[4,16]{1,0:T(4,128)S(1)}, s32[4,16]{1,0:T(4,128)}, u32[]{:S(2)}) copy-start(s32[4,16]{1,0:T(4,128)} %param.7) | copy-start | bytes 772
  61.5 53.6 %all-to-all-start.2 = ((bf16[4,512,1024]{2,1,0:T(8,128)(2,1)}), bf16[4,512,1024]{2,1,0:T(8,128)(2,1)}, u32[]{:S(2)}, u32[]{:S(2)}) async-start(bf16[4,512,1024]{2,1,0:T(8,128)(2,1)} %stack.4), calls=%async_computation.2 | async-start | bytes 8388608 | tf_op jit(solution)/shard_map/all_to_all | solution.py:57
  121.4 50.2 %copy-start.1 = (bf16[4,16,128,128]{3,1,2,0:T(8,128)(2,1)S(1)}, bf16[4,16,128,128]{3,1,2,0:T(8,128)(2,1)}, u32[]{:S(2)}) copy-start(bf16[4,16,128,128]{3,1,2,0:T(8,128)(2,1)} %get-tuple-element.10) | copy-start | bytes 6291460
  121.5 50.1 %copy-start.2 = (f32[512,1024]{1,0:T(8,128)S(1)}, f32[512,1024]{1,0:T(8,128)}, u32[]{:S(2)}) copy-start(f32[512,1024]{1,0:T(8,128)} %get-tuple-element.8) | copy-start | bytes 6291460
